TPU v7x, 256 devices: a whole 4x4x8 slice. The times are simulated.
256 devices in a mesh: dom: 32 (over x, y, core), sub: 8 (over z).
Axes of the slice: x: 4, y: 4, z: 8, core: 2. Of those that a mesh axis runs over, the one named last changes fastest.
Arguments:
- points: bfloat16 [524288, 256], P(('dom', 'sub')), may hold values from -60 to 60
- cotangent: bfloat16 [524288, 256], P(('dom', 'sub')), may hold values from -6 to 6
- counts: int32 [32], replicated, may hold values from 8192 to 16384, as said below
- w_in: bfloat16 [256, 512], replicated, may hold values from -0.375 to 0.375
- w_temp: bfloat16 [256, 8], replicated, may hold values from -1 to 1
- slice_weight: bfloat16 [8, 32, 64], replicated, may hold values from -2 to 2
- qkv_weight: float32 [3, 32, 32], replicated, may hold values from -1.5 to 1.5
- w_out: bfloat16 [256, 256], replicated, may hold values from -0.75 to 0.75
- b_out: float32 [256], replicated, may hold values from -3 to 3
Outputs:
- result: bfloat16 [524288, 256], P(('dom', 'sub'))
- grad_points: bfloat16 [524288, 256], P(('dom', 'sub'))
- grad_w_in: float32 [256, 512], replicated
- grad_w_temp: float32 [256, 8], replicated
- grad_slice: float32 [8, 32, 64], replicated
- grad_w_out: float32 [256, 256], replicated
- grad_bias: float32 [256], replicated
- grad_qkv: float32 [3, 32, 32], replicated
Inputs may be any that keep to these rules, and one draw needn't show every extreme that they name: `counts`: every count is a multiple of 128 and at least half of 16384 rounded down to tiles of 128; some partition is full in every draw.
All inputs are finite; a program needn't handle non-finite values.
Results may differ from a plain program's by a relative error of at most 0.015.
The roundings to bfloat16 on the way count: a program that leaves them out, or rounds other values in their place, can miss the bound.
Values sent between devices are 32-bit elements; how exact they have to be, the bound alone decides.
No kernel may reach another device: no remote copies, remote signals or barrier semaphores. Data moves between devices by JAX's collectives and lax.ppermute only.
A program may use at most 64 MiB of HBM per device.

v0:
```python
import jax
import jax.numpy as jnp
from jax import lax
from jax.experimental import pallas as pl
from jax.experimental.pallas import tpu as pltpu
from jax.sharding import Mesh, PartitionSpec as P

EPSILON = 1e-05
F32 = jnp.float32
BF16 = jnp.bfloat16
HIGH = lax.Precision.HIGHEST

D = 256
HEADS = 8
SLICES = 64
WIDTH = 32
ROWS = 2048
SUBS = 8
HALF = 896
VMEM_LIMIT = 40 * 1024 * 1024
SMALL_LIMIT = 16 * 1024 * 1024


def nn(a, b, precision=None):
    return lax.dot_general(
        a, b, (((1,), (0,)), ((), ())), preferred_element_type=F32, precision=precision
    )


def nt(a, b, precision=None):
    return lax.dot_general(
        a, b, (((1,), (1,)), ((), ())), preferred_element_type=F32, precision=precision
    )


def tn(a, b, precision=None):
    return lax.dot_general(
        a, b, (((0,), (0,)), ((), ())), preferred_element_type=F32, precision=precision
    )


def lane_ids(shape):
    return lax.broadcasted_iota(jnp.int32, shape, 1)


def device_place():
    x, y = lax.axis_index("x"), lax.axis_index("y")
    core, sub = lax.axis_index("core"), lax.axis_index("sub")
    return (x * 4 + y) * 2 + core, sub, core


def live_rows(counts_ref):
    dom, sub, _ = device_place()
    return counts_ref[dom] - sub * ROWS


def in_hbm(*arrays):
    return [pltpu.with_memory_space_constraint(a, pltpu.HBM) for a in arrays]


def inside_row(counts_ref):
    return jnp.where(lane_ids((1, ROWS)) < live_rows(counts_ref), 1.0, 0.0).astype(F32)


def forward_kernel(
    counts_ref,
    points_ref,
    cot_ref,
    w_in_ref,
    w_temp_ref,
    sw_ref,
    w_out_ref,
    packed_ref,
    fx_ref,
    gate_ref,
    top_ref,
    scale_ref,
    fb_ref,
    sw_cols_ref,
    w_all_t,
    sw_pad,
):
    w_all_t[0 : 2 * D, :] = w_in_ref[...].astype(F32).T.astype(BF16)
    w_all_t[2 * D :, :] = jnp.concatenate([w_temp_ref[...], jnp.zeros((8, D), BF16)], axis=0)
    for group in range(2):
        sw_pad[...] = jnp.zeros_like(sw_pad)
        for j in range(4):
            sw_pad[32 * j : 32 * j + 32, 64 * j : 64 * j + 64] = sw_ref[4 * group + j].astype(F32)
        sw_cols_ref[group] = sw_pad[...].T.astype(BF16)
    inside = inside_row(counts_ref)
    projected = nt(w_all_t[...], points_ref[...])
    gate = jax.nn.sigmoid(projected[2 * D : 2 * D + HEADS])
    gate_ref[...] = gate
    inv_temper = 1.0 / (0.5 + 1.5 * gate)
    proj_x = projected[0:D].astype(BF16)
    fx_ref[...] = proj_x
    for h in range(HEADS):
        fb_ref[64 * h + 32 : 64 * h + 64, :] = projected[D + 32 * h : D + 32 * h + 32].astype(BF16)
    back = (nt(w_out_ref[...], cot_ref[...]) * inside).astype(BF16)
    for h in range(HEADS):
        fb_ref[64 * h : 64 * h + 32, :] = back[32 * h : 32 * h + 32]
    sums = []
    folds = []
    for group in range(2):
        raw = nn(sw_cols_ref[group], proj_x[128 * group : 128 * group + 128])
        pieces = []
        for j in range(4):
            h = 4 * group + j
            logits = raw[64 * j : 64 * j + 64] * inv_temper[h : h + 1]
            top = jnp.max(logits, axis=0, keepdims=True)
            ex = jnp.exp(logits - top)
            scale = 1.0 / jnp.sum(ex, axis=0, keepdims=True)
            top_ref[h : h + 1, :] = top
            scale_ref[h : h + 1, :] = scale
            shares = ex * scale
            masked = shares * inside
            folded = masked[:, 0:128]
            for k in range(1, ROWS // 128):
                folded = folded + masked[:, 128 * k : 128 * k + 128]
            folds.append(folded)
            pieces.append(masked.astype(BF16))
        rounded = jnp.concatenate(pieces, axis=0)
        sums.append(nt(rounded, fb_ref[256 * group : 256 * group + 256, :]))
    low = lane_ids((32, 128)) < 64
    totals = nt(jnp.ones((8, 128), F32), jnp.concatenate(folds, axis=0), HIGH)
    for h in range(HEADS):
        group, j = divmod(h, 4)
        lanes = 128 * (j // 2)
        block = sums[group][64 * j : 64 * j + 64, lanes : lanes + 128]
        upper, lower = block[0:32], block[32:64]
        row = totals[:, 128 * (h // 2) : 128 * (h // 2) + 128]
        if j % 2 == 0:
            both = jnp.where(low, upper, pltpu.roll(lower, 64, 1))
        else:
            both = jnp.where(low, pltpu.roll(upper, 64, 1), lower)
            row = pltpu.roll(row, 64, 1)
        packed_ref[h, 0:32, :] = both
        packed_ref[h, 32:40, :] = row


def forward_call(counts, points, cotangent, w_in, w_temp, slice_weight, w_out):
    whole = pl.BlockSpec(memory_space=pltpu.VMEM)
    far = pl.BlockSpec(memory_space=pltpu.HBM)
    block = pl.BlockSpec()
    return pl.pallas_call(
        forward_kernel,
        in_specs=[pl.BlockSpec(memory_space=pltpu.SMEM)] + [block] * 6,
        out_specs=[whole] * 6,
        out_shape=[
            jax.ShapeDtypeStruct((HEADS, 40, 128), F32),
            jax.ShapeDtypeStruct((D, ROWS), BF16),
            jax.ShapeDtypeStruct((HEADS, ROWS), F32),
            jax.ShapeDtypeStruct((HEADS, ROWS), F32),
            jax.ShapeDtypeStruct((HEADS, ROWS), F32),
            jax.ShapeDtypeStruct((2 * D, ROWS), BF16),
        ],
        scratch_shapes=[
            pltpu.VMEM((2, 256, 128), BF16),
            pltpu.VMEM((2 * D + 16, D), BF16),
            pltpu.VMEM((128, 256), F32),
        ],
        compiler_params=pltpu.CompilerParams(vmem_limit_bytes=VMEM_LIMIT),
        name="forward",
    )(*in_hbm(counts, points, cotangent, w_in, w_temp.T, slice_weight, w_out))


def attention_kernel(parts_ref, qkv_ref, out_ref, grad_qkv_ref):
    summed = parts_ref[0]
    for k in range(1, parts_ref.shape[0]):
        summed = summed + parts_ref[k]
    pairs = jnp.concatenate([summed[0:32], pltpu.roll(summed[0:32], 64, 1)], axis=0)
    grad_att = pairs[:, 0:WIDTH]
    numer = pltpu.roll(pairs, 96, 1)[:, 0:WIDTH]
    totals = jnp.concatenate([summed[32:40]] * 16, axis=0).T[0:SLICES, 0:1]
    inv = 1.0 / (totals + EPSILON)
    tokens = numer * inv
    w_q, w_k, w_v = qkv_ref[0], qkv_ref[1], qkv_ref[2]
    scale = WIDTH**-0.5
    query = nn(tokens, w_q, HIGH)
    keys = nn(tokens, w_k, HIGH)
    values = nn(tokens, w_v, HIGH)
    scores = nt(query, keys, HIGH) * scale
    ex = jnp.exp(scores - jnp.max(scores, axis=1, keepdims=True))
    weights = ex / jnp.sum(ex, axis=1, keepdims=True)
    attended = nn(weights, values, HIGH)
    grad_values = tn(weights, grad_att, HIGH)
    grad_weights = nt(grad_att, values, HIGH)
    inner = jnp.sum(weights * grad_weights, axis=1, keepdims=True)
    grad_scores = weights * (grad_weights - inner) * scale
    grad_query = nn(grad_scores, keys, HIGH)
    grad_keys = tn(grad_scores, query, HIGH)
    grad_tokens = (
        nt(grad_query, w_q, HIGH) + nt(grad_keys, w_k, HIGH) + nt(grad_values, w_v, HIGH)
    )
    grad_qkv_ref[...] = jnp.zeros_like(grad_qkv_ref)
    for i, grad in enumerate((grad_query, grad_keys, grad_values)):
        grad_qkv_ref[:, WIDTH * i : WIDTH * i + WIDTH] = tn(tokens, grad, HIGH) * (1.0 / 32)
    grad_numer = grad_tokens * inv
    grad_totals = -jnp.sum(grad_tokens * tokens, axis=1, keepdims=True) * inv
    grad_row = jnp.broadcast_to(grad_totals, (SLICES, 128)).T[0:8]
    for k in range(out_ref.shape[0]):
        out_ref[k, 0:32, 0:32] = attended[0:32]
        out_ref[k, 0:32, 32:64] = grad_numer[0:32]
        out_ref[k, 0:32, 64:96] = attended[32:64]
        out_ref[k, 0:32, 96:128] = grad_numer[32:64]
        out_ref[k, 32:40, 0:64] = grad_row
        out_ref[k, 32:40, 64:128] = grad_row


def attention_call(parts, qkv_weight):
    whole = pl.BlockSpec(memory_space=pltpu.VMEM)
    return pl.pallas_call(
        attention_kernel,
        in_specs=[whole, whole],
        out_specs=[whole, whole],
        out_shape=[
            jax.ShapeDtypeStruct((SUBS, 40, 128), F32),
            jax.ShapeDtypeStruct((WIDTH, 128), F32),
        ],
        compiler_params=pltpu.CompilerParams(vmem_limit_bytes=SMALL_LIMIT),
        name="slice_attention",
    )(parts, qkv_weight)


def backward_kernel(
    counts_ref,
    points_hbm,
    cot_hbm,
    fx_ref,
    gate_ref,
    top_ref,
    scale_ref,
    fb_ref,
    sw_ref,
    w_in_ref,
    w_temp_ref,
    w_out_ref,
    b_out_ref,
    heads_ref,
    grad_qkv_ref,
    result_hbm,
    grad_points_hbm,
    mine_ref,
    theirs_ref,
    result_ref,
    grad_points_ref,
    mixed_ref,
    proj_ref,
    points_ref,
    cot_ref,
    sw_rows_ref,
    token_pad,
    token_cols,
    token_rows,
    grad_tot,
    sems,
):
    get_points = pltpu.make_async_copy(points_hbm, points_ref, sems.at[0])
    get_cot = pltpu.make_async_copy(cot_hbm, cot_ref, sems.at[1])
    put_result = pltpu.make_async_copy(result_ref, result_hbm, sems.at[2])
    put_grad = pltpu.make_async_copy(grad_points_ref, grad_points_hbm, sems.at[3])
    get_points.start()
    get_cot.start()
    sw_rows_ref[...] = jnp.zeros_like(sw_rows_ref)
    for h in range(HEADS):
        group, j = divmod(h, 4)
        sw_rows_ref[group, 32 * j : 32 * j + 32, 64 * j : 64 * j + 64] = sw_ref[h]
    rows = [heads_ref[h, 32:33, :] for h in range(HEADS)]
    square = jnp.concatenate(rows * 16, axis=0).T
    low = lane_ids((64, 128)) < 64
    for group in range(2):
        token_pad[...] = jnp.zeros_like(token_pad)
        for j in range(4):
            h = 4 * group + j
            both = heads_ref[h, 0:32, :]
            turned = pltpu.roll(both, 64, 1)
            lanes = 128 * (j // 2)
            if j % 2 == 0:
                block = jnp.where(low, jnp.concatenate([both, turned], axis=0), 0.0)
            else:
                block = jnp.where(low, 0.0, jnp.concatenate([turned, both], axis=0))
            token_pad[64 * j : 64 * j + 64, lanes : lanes + 128] = block
            grad_tot[64 * h : 64 * h + 64, :] = jnp.broadcast_to(square[0:64, h : h + 1], (64, 128))
        token_cols[group] = token_pad[...].astype(BF16)
        token_rows[group] = token_pad[...].T.astype(BF16)

    inside = inside_row(counts_ref)
    gate = gate_ref[...]
    inv_temper = 1.0 / (0.5 + 1.5 * gate)
    scale_temp = -1.5 * gate * (1.0 - gate) * inv_temper
    b_col = jnp.broadcast_to(b_out_ref[...], (128, D)).T[:, 0:1]
    w_out_t = w_out_ref[...].astype(F32).T.astype(BF16)
    temp_cols = jnp.concatenate([w_temp_ref[...].astype(F32), jnp.zeros((120, D), F32)], axis=0).T
    temp_cols = temp_cols[:, 0:16].astype(BF16)
    temp_rows = []
    slices = []
    for group in range(2):
        fx = fx_ref[128 * group : 128 * group + 128, :]
        raw = tn(sw_rows_ref[group], fx)
        total = nn(token_cols[group], fb_ref[256 * group : 256 * group + 256, :])
        scaled_parts = []
        rounded_parts = []
        for j in range(4):
            h = 4 * group + j
            rows = slice(64 * j, 64 * j + 64)
            logits = raw[rows] * inv_temper[h : h + 1]
            shares = jnp.exp(logits - top_ref[h : h + 1, :]) * scale_ref[h : h + 1, :]
            gt = grad_tot[64 * h : 64 * h + 64, :]
            share_grad = total[rows] + jnp.concatenate([gt] * (ROWS // 128), axis=1)
            inner = jnp.sum(shares * share_grad, axis=0, keepdims=True)
            scaled = shares * (share_grad - inner) * (inside * inv_temper[h : h + 1])
            temp_rows.append(
                jnp.sum(scaled * raw[rows], axis=0, keepdims=True) * scale_temp[h : h + 1]
            )
            scaled_parts.append(scaled.astype(BF16))
            rounded_parts.append((shares * inside).astype(BF16))
        scaled_bf = jnp.concatenate(scaled_parts, axis=0)
        slices.append(nt(fx, scaled_bf))
        proj_ref[128 * group : 128 * group + 128, :] = nn(sw_rows_ref[group], scaled_bf).astype(
            BF16
        )
        pair = nn(token_rows[group], jnp.concatenate(rounded_parts, axis=0)).astype(BF16)
        for j in range(4):
            h = 4 * group + j
            mixed_ref[32 * h : 32 * h + 32, :] = pair[64 * j : 64 * j + 32]
            proj_ref[D + 32 * h : D + 32 * h + 32, :] = pair[64 * j + 32 : 64 * j + 64]
    mixed_ref[D:, :] = jnp.broadcast_to(inside, (16, ROWS)).astype(BF16)
    out = nn(w_out_t, mixed_ref[0:D, :]) + b_col
    result_ref[...] = (out * inside).astype(BF16).T
    proj_ref[2 * D :, :] = jnp.concatenate(
        temp_rows + [jnp.zeros((8, ROWS), F32)], axis=0
    ).astype(BF16)
    grad = nn(w_in_ref[...], proj_ref[0 : 2 * D, :]) + nn(temp_cols, proj_ref[2 * D :, :])
    grad_points_ref[...] = grad.astype(BF16).T
    put_result.start()
    put_grad.start()
    get_points.wait()
    get_cot.wait()
    sum_out = nn(mixed_ref[...], cot_ref[...])
    sum_in = nn(proj_ref[...], points_ref[...])
    turned_in = [sum_in[128 * k : 128 * k + 128, :].T for k in range(4)]
    low = lane_ids((32, 128)) < 64

    def write_first(ref):
        for k in range(3):
            ref[256 * k : 256 * k + 256, :] = turned_in[k]
        for k in range(4):
            group, pair = divmod(k, 2)
            block = slices[group][64 * pair : 64 * pair + 64, 128 * pair : 128 * pair + 128]
            ref[768 + 32 * k : 800 + 32 * k, :] = jnp.where(low, block[0:32], block[32:64])

    def write_second(ref):
        ref[0:256, :] = turned_in[3]
        ref[256:512, :] = sum_out[0:256, 0:128]
        ref[512:768, :] = sum_out[0:256, 128:256]
        ref[768:776, :] = sum_in[512:520, 0:128]
        ref[776:784, :] = sum_in[512:520, 128:256]
        ref[784:792, :] = sum_out[256:264, 0:128]
        ref[792:800, :] = sum_out[256:264, 128:256]
        ref[800:832, :] = grad_qkv_ref[...]
        ref[832:HALF, :] = jnp.zeros((HALF - 832, 128), F32)

    core = device_place()[2]

    @pl.when(core == 0)
    def _():
        write_first(mine_ref)
        write_second(theirs_ref)

    @pl.when(core != 0)
    def _():
        write_first(theirs_ref)
        write_second(mine_ref)

    put_result.wait()
    put_grad.wait()


def backward_call(
    counts, points, cotangent, stash, heads, grad_qkv, w_in, w_temp, slice_weight, w_out, b_out
):
    whole = pl.BlockSpec(memory_space=pltpu.VMEM)
    far = pl.BlockSpec(memory_space=pltpu.HBM)
    block = pl.BlockSpec()
    return pl.pallas_call(
        backward_kernel,
        in_specs=[pl.BlockSpec(memory_space=pltpu.SMEM), far, far] + [whole] * 5
        + [block] * 5
        + [whole, whole],
        out_specs=[far, far, whole, whole],
        out_shape=[
            pltpu.HBM((ROWS, D), BF16),
            pltpu.HBM((ROWS, D), BF16),
            jax.ShapeDtypeStruct((HALF, 128), F32),
            jax.ShapeDtypeStruct((HALF, 128), F32),
        ],
        scratch_shapes=[
            pltpu.VMEM((ROWS, D), BF16),
            pltpu.VMEM((ROWS, D), BF16),
            pltpu.VMEM((D + 16, ROWS), BF16),
            pltpu.VMEM((2 * D + 16, ROWS), BF16),
            pltpu.VMEM((ROWS, D), BF16),
            pltpu.VMEM((ROWS, D), BF16),
            pltpu.VMEM((2, 128, 256), BF16),
            pltpu.VMEM((256, 256), F32),
            pltpu.VMEM((2, 256, 256), BF16),
            pltpu.VMEM((2, 256, 256), BF16),
            pltpu.VMEM((2 * D, 128), F32),
            pltpu.SemaphoreType.DMA((4,)),
        ],
        compiler_params=pltpu.CompilerParams(vmem_limit_bytes=VMEM_LIMIT),
        name="backward",
    )(
        *in_hbm(counts, points, cotangent),
        *stash,
        *in_hbm(slice_weight, w_in, w_temp.T, w_out, b_out.reshape(1, D)),
        heads,
        grad_qkv,
    )


def sum_spread(parts, copies):
    summed = jnp.sum(parts, axis=0)
    return jnp.broadcast_to(summed[None], (copies,) + summed.shape)


def unpack_kernel(
    mine_ref,
    theirs_ref,
    grad_in_ref,
    grad_temp_ref,
    grad_slice_ref,
    grad_out_ref,
    grad_bias_ref,
    grad_qkv_ref,
):
    def unpack(first, second):
        for k in range(3):
            grad_in_ref[:, 128 * k : 128 * k + 128] = first[256 * k : 256 * k + 256, :]
        grad_in_ref[:, 384:512] = second[0:256, :]
        for k in range(4):
            block = first[768 + 32 * k : 800 + 32 * k, :]
            grad_slice_ref[2 * k] = block[:, 0:64]
            grad_slice_ref[2 * k + 1] = pltpu.roll(block, 64, 1)[:, 0:64]
        grad_out_ref[:, 0:128] = second[256:512, :]
        grad_out_ref[:, 128:256] = second[512:768, :]
        for k in range(2):
            rows = second[768 + 8 * k : 776 + 8 * k, :]
            grad_temp_ref[:, 128 * k : 128 * k + 128] = rows
            grad_bias_ref[0:1, 128 * k : 128 * k + 128] = second[784 + 8 * k : 785 + 8 * k, :]
        qkv = second[800:832, :]
        grad_qkv_ref[0] = qkv[:, 0:32]
        grad_qkv_ref[1] = pltpu.roll(qkv, 96, 1)[:, 0:32]
        grad_qkv_ref[2] = pltpu.roll(qkv, 64, 1)[:, 0:32]

    core = device_place()[2]

    @pl.when(core == 0)
    def _():
        unpack(mine_ref, theirs_ref)

    @pl.when(core != 0)
    def _():
        unpack(theirs_ref, mine_ref)


def unpack_call(mine, theirs):
    whole = pl.BlockSpec(memory_space=pltpu.VMEM)
    return pl.pallas_call(
        unpack_kernel,
        in_specs=[whole, whole],
        out_specs=[whole] * 6,
        out_shape=[
            jax.ShapeDtypeStruct((D, 2 * D), F32),
            jax.ShapeDtypeStruct((HEADS, D), F32),
            jax.ShapeDtypeStruct((HEADS, WIDTH, SLICES), F32),
            jax.ShapeDtypeStruct((D, D), F32),
            jax.ShapeDtypeStruct((1, D), F32),
            jax.ShapeDtypeStruct((3, WIDTH, WIDTH), F32),
        ],
        compiler_params=pltpu.CompilerParams(vmem_limit_bytes=SMALL_LIMIT),
        name="unpack",
    )(mine, theirs)


def swap_cores(values):
    return lax.ppermute(values, "core", [(0, 1), (1, 0)])


def spread_over(values, axes):
    return lax.all_to_all(values, axes, 0, 0)


def per_device(points, cotangent, counts, w_in, w_temp, slice_weight, qkv_weight, w_out, b_out):
    packed, *stash = forward_call(counts, points, cotangent, w_in, w_temp, slice_weight, w_out)
    packed = packed + swap_cores(packed)
    parts = sum_spread(spread_over(packed, "sub"), 16)
    parts = spread_over(parts, ("x", "y"))
    heads, grad_qkv = attention_call(parts, qkv_weight)
    heads = spread_over(heads, "sub")
    result, grad_points, mine, theirs = backward_call(
        counts,
        points,
        cotangent,
        stash,
        heads,
        grad_qkv,
        w_in,
        w_temp,
        slice_weight,
        w_out,
        b_out,
    )
    mine = (mine + swap_cores(theirs)).reshape(16, HALF // 16, 128)
    mine = sum_spread(spread_over(mine, ("x", "y")), SUBS)
    mine = sum_spread(spread_over(mine, "sub"), 16)
    mine = spread_over(mine, ("x", "y")).reshape(HALF, 128)
    theirs = swap_cores(mine)
    grad_w_in, grad_w_temp, grad_slice, grad_w_out, grad_bias, grad_qkv = unpack_call(mine, theirs)
    return (
        result,
        grad_points,
        grad_w_in,
        grad_w_temp.T,
        grad_slice,
        grad_w_out,
        grad_bias.reshape(D),
        grad_qkv,
    )


def solution(mesh):
    fine = Mesh(mesh.devices.reshape(4, 4, 2, 8), ("x", "y", "core", "sub"))
    rows = P(("x", "y", "core", "sub"), None)
    return jax.shard_map(
        per_device,
        mesh=fine,
        in_specs=(rows, rows) + (P(),) * 7,
        out_specs=(rows, rows) + (P(),) * 6,
        check_vma=False,
    )
```

profile of v0, /device:TPU:1, one launch (start us, length us, event | category | flops | bytes accessed | tf_op | source)
XLA Modules:
  0.0 109.8 jit_solution(2513483980063372408)
XLA Ops:
  0.6 0.0 copy-start
  0.6 4.9 %forward.1 = (f32[8,40,128]{2,1,0:T(8,128)S(1)}, bf16[256,2048]{1,0:T(8,128)(2,1)S(1)}, f32[8,2048]{1,0:T(8,128)S(1)}, f32[8,2048]{1,0:T(8,128)S(1)}, f32[8,2048...) custom-call(s32[32]{0:T(128)} %counts_ref.3, bf16[2048,256]{1,0:T(8,128)(2,1)} %points_hbm.1, bf16[2048,256]{1,0:T(8,128)(2,1)} %cot_hbm.1, ...), custom_call_target="tpu_custom_call" | custom-call | tf_op jit(solution)/shard_map/forward/pallas_call | solution.py:145
  5.5 3.3 %collective-permute-start = (f32[8,40,128]{2,1,0:T(8,128)S(1)}, f32[8,40,128]{2,1,0:T(8,128)S(1)}, u32[]{:S(2)}, u32[]{:S(2)}) collective-permute-start(f32[8,40,128]{2,1,0:T(8,128)S(1)} %get-tuple-element.31), channel_id=1, source_target_pairs={{0,8},{8,0},{1,9},{9,1},{2,10},{10,2},{3,11},{11,3},{4,12},{12,4},... | collective-permute-start | bytes 491528 | tf_op jit(solution)/shard_map/ppermute | solution.py:487
  8.9 1.0 collective-permute-done
  9.9 14.9 %all_to_all.30 = f32[8,40,128]{2,1,0:T(8,128)S(1)} all-to-all(f32[8,40,128]{2,1,0:T(8,128)S(1)} %add.6), channel_id=1, replica_groups=mesh['x'=4,'y'=4,'core'=2,'sub'=8] {'sub'}, dimensions={0} | all-to-all | bytes 327680 | tf_op jit(solution)/shard_map/all_to_all | solution.py:491
  24.8 0.6 reduce_sum.27
  25.4 0.7 broadcast_in_dim.6
  26.2 14.2 %all_to_all.31.parts_ref = f32[16,40,128]{2,1,0:T(8,128)S(1)} all-to-all(f32[16,40,128]{2,1,0:T(8,128)S(1)} %broadcast_in_dim.6), channel_id=1, replica_groups=mesh['x'=4,'y'=4,'core'=2,'sub'=8] {'x','y'}, dimensions={0} | all-to-all | bytes 655360 | tf_op jit(solution)/shard_map/all_to_all | solution.py:491
  40.4 0.0 copy-done
  40.4 1.6 %slice_attention.1 = (f32[8,40,128]{2,1,0:T(8,128)S(1)}, f32[32,128]{1,0:T(8,128)S(1)}) custom-call(f32[16,40,128]{2,1,0:T(8,128)S(1)} %all_to_all.31.parts_ref, f32[3,32,32]{2,1,0:T(8,128)S(1)} %copy-done), custom_call_target="tpu_custom_call" | custom-call | tf_op jit(solution)/shard_map/slice_attention/pallas_call | solution.py:212
  42.0 11.0 %all_to_all.32.heads_ref = f32[8,40,128]{2,1,0:T(8,128)S(1)} all-to-all(f32[8,40,128]{2,1,0:T(8,128)S(1)} %get-tuple-element.32), channel_id=1, replica_groups=mesh['x'=4,'y'=4,'core'=2,'sub'=8] {'sub'}, dimensions={0} | all-to-all | bytes 327680 | tf_op jit(solution)/shard_map/all_to_all | solution.py:491
  53.0 7.3 %backward.1 = (bf16[2048,256]{1,0:T(8,128)(2,1)}, bf16[2048,256]{1,0:T(8,128)(2,1)}, f32[896,128]{1,0:T(8,128)S(1)}, f32[896,128]{1,0:T(8,128)S(1)}) custom-call(s32[32]{0:T(128)} %counts_ref.3, bf16[2048,256]{1,0:T(8,128)(2,1)} %points_hbm.1, bf16[2048,256]{1,0:T(8,128)(2,1)} %cot_hbm.1, bf16[256,2048]{1,0:T(8,128)(2,1)S(1)} %get-tuple-element.26.fx_ref, ...), custom_call_target="tpu_custom_call" | custom-call | tf_op jit(solution)/shard_map/backward/pallas_call | solution.py:385
  60.3 4.5 %collective-permute-start.1 = (f32[896,128]{1,0:T(8,128)S(1)}, f32[896,128]{1,0:T(8,128)S(1)}, u32[]{:S(2)}, u32[]{:S(2)}) collective-permute-start(f32[896,128]{1,0:T(8,128)S(1)} %get-tuple-element.37), channel_id=1, source_target_pairs={{0,8},{8,0},{1,9},{9,1},{2,10},{10,2},{3,11},{11,3},{4,12},{12,4},... | collective-permute-start | bytes 1376264 | tf_op jit(solution)/shard_map/ppermute | solution.py:487
  64.8 1.4 %collective-permute-done.1 = f32[896,128]{1,0:T(8,128)S(1)} collective-permute-done((f32[896,128]{1,0:T(8,128)S(1)}, f32[896,128]{1,0:T(8,128)S(1)}, u32[]{:S(2)}, u32[]{:S(2)}) %collective-permute-start.1) | collective-permute-done | bytes 458784 | tf_op jit(solution)/shard_map/ppermute | solution.py:487
  66.2 0.1 add.7
  66.3 13.0 %all_to_all.33 = f32[16,56,128]{2,1,0:T(8,128)S(1)} all-to-all(f32[16,56,128]{2,1,0:T(8,128)S(1)} %bitcast.8), channel_id=1, replica_groups=mesh['x'=4,'y'=4,'core'=2,'sub'=8] {'x','y'}, dimensions={0} | all-to-all | bytes 917504 | tf_op jit(solution)/shard_map/all_to_all | solution.py:491
  79.4 11.3 %all_to_all.34 = f32[8,56,128]{2,1,0:T(8,128)S(1)} all-to-all(f32[8,56,128]{2,1,0:T(8,128)S(1)} %broadcast_in_dim.7), channel_id=1, replica_groups=mesh['x'=4,'y'=4,'core'=2,'sub'=8] {'sub'}, dimensions={0} | all-to-all | bytes 458752 | tf_op jit(solution)/shard_map/all_to_all | solution.py:491
  90.7 12.3 %all_to_all.35 = f32[16,56,128]{2,1,0:T(8,128)S(1)} all-to-all(f32[16,56,128]{2,1,0:T(8,128)S(1)} %broadcast_in_dim.8), channel_id=1, replica_groups=mesh['x'=4,'y'=4,'core'=2,'sub'=8] {'x','y'}, dimensions={0} | all-to-all | bytes 917504 | tf_op jit(solution)/shard_map/all_to_all | solution.py:491
  103.0 4.3 %collective-permute-start.2 = (f32[896,128]{1,0:T(8,128)S(1)}, f32[896,128]{1,0:T(8,128)S(1)}, u32[]{:S(2)}, u32[]{:S(2)}) collective-permute-start(f32[896,128]{1,0:T(8,128)S(1)} %bitcast.6), channel_id=1, source_target_pairs={{0,8},{8,0},{1,9},{9,1},{2,10},{10,2},{3,11},{11,3},{4,12},{12,4},... | collective-permute-start | bytes 1376264 | tf_op jit(solution)/shard_map/ppermute | solution.py:487
  107.3 1.4 %collective-permute-done.2.theirs_ref = f32[896,128]{1,0:T(8,128)S(1)} collective-permute-done((f32[896,128]{1,0:T(8,128)S(1)}, f32[896,128]{1,0:T(8,128)S(1)}, u32[]{:S(2)}, u32[]{:S(2)}) %collective-permute-start.2) | collective-permute-done | bytes 458784 | tf_op jit(solution)/shard_map/ppermute | solution.py:487
  108.8 1.0 unpack.1
  (5 shorter events, 0.1 us)
Async XLA Ops:
  0.6 39.8 %copy-start = (f32[3,32,32]{2,1,0:T(8,128)S(1)}, f32[3,32,32]{2,1,0:T(8,128)}, u32[]{:S(2)}) copy-start(f32[3,32,32]{2,1,0:T(8,128)} %qkv_ref.1) | copy-start | bytes 36868
  5.5 4.4 %collective-permute-start = (f32[8,40,128]{2,1,0:T(8,128)S(1)}, f32[8,40,128]{2,1,0:T(8,128)S(1)}, u32[]{:S(2)}, u32[]{:S(2)}) collective-permute-start(f32[8,40,128]{2,1,0:T(8,128)S(1)} %get-tuple-element.31), channel_id=1, source_target_pairs={{0,8},{8,0},{1,9},{9,1},{2,10},{10,2},{3,11},{11,3},{4,12},{12,4},... | collective-permute-start | bytes 491528 | tf_op jit(solution)/shard_map/ppermute | solution.py:487
  60.3 5.9 %collective-permute-start.1 = (f32[896,128]{1,0:T(8,128)S(1)}, f32[896,128]{1,0:T(8,128)S(1)}, u32[]{:S(2)}, u32[]{:S(2)}) collective-permute-start(f32[896,128]{1,0:T(8,128)S(1)} %get-tuple-element.37), channel_id=1, source_target_pairs={{0,8},{8,0},{1,9},{9,1},{2,10},{10,2},{3,11},{11,3},{4,12},{12,4},... | collective-permute-start | bytes 1376264 | tf_op jit(solution)/shard_map/ppermute | solution.py:487
  103.0 5.8 %collective-permute-start.2 = (f32[896,128]{1,0:T(8,128)S(1)}, f32[896,128]{1,0:T(8,128)S(1)}, u32[]{:S(2)}, u32[]{:S(2)}) collective-permute-start(f32[896,128]{1,0:T(8,128)S(1)} %bitcast.6), channel_id=1, source_target_pairs={{0,8},{8,0},{1,9},{9,1},{2,10},{10,2},{3,11},{11,3},{4,12},{12,4},... | collective-permute-start | bytes 1376264 | tf_op jit(solution)/shard_map/ppermute | solution.py:487
where the time goes:
time: 110 us
  blocking collectives  76.7 us (70%)
  Pallas kernels  14.9 us (14%)
  starting transfers between devices  12.1 us (11%)
  waiting for transfers between devices  3.91 us (4%)
    all_to_all x6, blocking collectives, spread_over(): return lax.all_to_all(values, axes, 0, 0)  76.7 us
    ppermute x3, starting transfers between devices, swap_cores(): return lax.ppermute(values, 'core', [(0, 1), (1, 0)])  12.1 us
    pallas_call x1, Pallas kernels, backward_call(): pl.pallas_call(backward_kernel, in_specs=[pl.BlockSpec(memory_space=pltpu...  7.3 us
    pallas_call x1, Pallas kernels, forward_call(): pl.pallas_call(forward_kernel, in_specs=[pl.BlockSpec(memory_space=pltpu....  4.89 us
    ppermute x3, waiting for transfers between devices, swap_cores(): return lax.ppermute(values, 'core', [(0, 1), (1, 0)])  3.91 us
  transfers between devices with their start and end apart: 3, of which 3 were waited for; matrix products, arithmetic and copies ran while one was open for 0% of the time, Pallas kernels for 0%

commit v1 on v0

--- a/solution.py
+++ b/solution.py
@@ -420,7 +420,9 @@
 
 
 def sum_spread(parts, copies):
-    summed = jnp.sum(parts, axis=0)
+    summed = parts[0]
+    for k in range(1, parts.shape[0]):
+        summed = summed + parts[k]
     return jnp.broadcast_to(summed[None], (copies,) + summed.shape)
 
 

time: 110 us -> 109 us (level)
  no operation moved by 1% of the time
where the time goes in v1:
time: 109 us; the launch traced here: 108 us
  blocking collectives  76.7 us (70%)
  Pallas kernels  14.9 us (14%)
  starting transfers between devices  12.1 us (11%)
  waiting for transfers between devices  3.91 us (4%)
    all_to_all x6, blocking collectives, spread_over(): return lax.all_to_all(values, axes, 0, 0)  76.7 us
    ppermute x3, starting transfers between devices, swap_cores(): return lax.ppermute(values, 'core', [(0, 1), (1, 0)])  12.1 us
    pallas_call x1, Pallas kernels, backward_call(): pl.pallas_call(backward_kernel, in_specs=[pl.BlockSpec(memory_space=pltpu...  7.3 us
    pallas_call x1, Pallas kernels, forward_call(): pl.pallas_call(forward_kernel, in_specs=[pl.BlockSpec(memory_space=pltpu....  4.89 us
    ppermute x3, waiting for transfers between devices, swap_cores(): return lax.ppermute(values, 'core', [(0, 1), (1, 0)])  3.91 us
  transfers between devices with their start and end apart: 3, of which 3 were waited for; matrix products, arithmetic and copies ran while one was open for 0% of the time, Pallas kernels for 0%

profile of v1, /device:TPU:1, one launch (start us, length us, event | category | flops | bytes accessed | tf_op | source)
XLA Modules:
  0.0 108.5 jit_solution(1344969197203750766)
XLA Ops:
  0.6 0.0 copy-start
  0.6 4.9 %forward.1 = (f32[8,40,128]{2,1,0:T(8,128)S(1)}, bf16[256,2048]{1,0:T(8,128)(2,1)S(1)}, f32[8,2048]{1,0:T(8,128)S(1)}, f32[8,2048]{1,0:T(8,128)S(1)}, f32[8,2048...) custom-call(s32[32]{0:T(128)} %counts_ref.3, bf16[2048,256]{1,0:T(8,128)(2,1)} %points_hbm.1, bf16[2048,256]{1,0:T(8,128)(2,1)} %cot_hbm.1, ...), custom_call_target="tpu_custom_call" | custom-call | tf_op jit(solution)/shard_map/forward/pallas_call | solution.py:145
  5.5 3.3 %collective-permute-start = (f32[8,40,128]{2,1,0:T(8,128)S(1)}, f32[8,40,128]{2,1,0:T(8,128)S(1)}, u32[]{:S(2)}, u32[]{:S(2)}) collective-permute-start(f32[8,40,128]{2,1,0:T(8,128)S(1)} %get-tuple-element.31), channel_id=1, source_target_pairs={{0,8},{8,0},{1,9},{9,1},{2,10},{10,2},{3,11},{11,3},{4,12},{12,4},... | collective-permute-start | bytes 491528 | tf_op jit(solution)/shard_map/ppermute | solution.py:489
  8.9 1.0 collective-permute-done
  9.9 14.9 %all_to_all.30 = f32[8,40,128]{2,1,0:T(8,128)S(1)} all-to-all(f32[8,40,128]{2,1,0:T(8,128)S(1)} %add.122), channel_id=1, replica_groups=mesh['x'=4,'y'=4,'core'=2,'sub'=8] {'sub'}, dimensions={0} | all-to-all | bytes 327680 | tf_op jit(solution)/shard_map/all_to_all | solution.py:493
  24.8 14.2 %all_to_all.31.parts_ref = f32[16,40,128]{2,1,0:T(8,128)S(1)} all-to-all(f32[16,40,128]{2,1,0:T(8,128)S(1)} %broadcast_in_dim.25), channel_id=1, replica_groups=mesh['x'=4,'y'=4,'core'=2,'sub'=8] {'x','y'}, dimensions={0} | all-to-all | bytes 655360 | tf_op jit(solution)/shard_map/all_to_all | solution.py:493
  39.1 0.0 copy-done
  39.1 1.6 %slice_attention.1 = (f32[8,40,128]{2,1,0:T(8,128)S(1)}, f32[32,128]{1,0:T(8,128)S(1)}) custom-call(f32[16,40,128]{2,1,0:T(8,128)S(1)} %all_to_all.31.parts_ref, f32[3,32,32]{2,1,0:T(8,128)S(1)} %copy-done), custom_call_target="tpu_custom_call" | custom-call | tf_op jit(solution)/shard_map/slice_attention/pallas_call | solution.py:212
  40.7 11.0 %all_to_all.32.heads_ref = f32[8,40,128]{2,1,0:T(8,128)S(1)} all-to-all(f32[8,40,128]{2,1,0:T(8,128)S(1)} %get-tuple-element.32), channel_id=1, replica_groups=mesh['x'=4,'y'=4,'core'=2,'sub'=8] {'sub'}, dimensions={0} | all-to-all | bytes 327680 | tf_op jit(solution)/shard_map/all_to_all | solution.py:493
  51.7 7.3 %backward.1 = (bf16[2048,256]{1,0:T(8,128)(2,1)}, bf16[2048,256]{1,0:T(8,128)(2,1)}, f32[896,128]{1,0:T(8,128)S(1)}, f32[896,128]{1,0:T(8,128)S(1)}) custom-call(s32[32]{0:T(128)} %counts_ref.3, bf16[2048,256]{1,0:T(8,128)(2,1)} %points_hbm.1, bf16[2048,256]{1,0:T(8,128)(2,1)} %cot_hbm.1, bf16[256,2048]{1,0:T(8,128)(2,1)S(1)} %get-tuple-element.26.fx_ref, ...), custom_call_target="tpu_custom_call" | custom-call | tf_op jit(solution)/shard_map/backward/pallas_call | solution.py:385
  59.0 4.5 %collective-permute-start.1 = (f32[896,128]{1,0:T(8,128)S(1)}, f32[896,128]{1,0:T(8,128)S(1)}, u32[]{:S(2)}, u32[]{:S(2)}) collective-permute-start(f32[896,128]{1,0:T(8,128)S(1)} %get-tuple-element.37), channel_id=1, source_target_pairs={{0,8},{8,0},{1,9},{9,1},{2,10},{10,2},{3,11},{11,3},{4,12},{12,4},... | collective-permute-start | bytes 1376264 | tf_op jit(solution)/shard_map/ppermute | solution.py:489
  63.4 1.4 %collective-permute-done.1 = f32[896,128]{1,0:T(8,128)S(1)} collective-permute-done((f32[896,128]{1,0:T(8,128)S(1)}, f32[896,128]{1,0:T(8,128)S(1)}, u32[]{:S(2)}, u32[]{:S(2)}) %collective-permute-start.1) | collective-permute-done | bytes 458784 | tf_op jit(solution)/shard_map/ppermute | solution.py:489
  64.9 0.1 add.130
  64.9 13.0 %all_to_all.33 = f32[16,56,128]{2,1,0:T(8,128)S(1)} all-to-all(f32[16,56,128]{2,1,0:T(8,128)S(1)} %bitcast.14), channel_id=1, replica_groups=mesh['x'=4,'y'=4,'core'=2,'sub'=8] {'x','y'}, dimensions={0} | all-to-all | bytes 917504 | tf_op jit(solution)/shard_map/all_to_all | solution.py:493
  78.0 11.3 %all_to_all.34 = f32[8,56,128]{2,1,0:T(8,128)S(1)} all-to-all(f32[8,56,128]{2,1,0:T(8,128)S(1)} %broadcast_in_dim.27), channel_id=1, replica_groups=mesh['x'=4,'y'=4,'core'=2,'sub'=8] {'sub'}, dimensions={0} | all-to-all | bytes 458752 | tf_op jit(solution)/shard_map/all_to_all | solution.py:493
  89.4 12.3 %all_to_all.35 = f32[16,56,128]{2,1,0:T(8,128)S(1)} all-to-all(f32[16,56,128]{2,1,0:T(8,128)S(1)} %broadcast_in_dim.29), channel_id=1, replica_groups=mesh['x'=4,'y'=4,'core'=2,'sub'=8] {'x','y'}, dimensions={0} | all-to-all | bytes 917504 | tf_op jit(solution)/shard_map/all_to_all | solution.py:493
  101.7 4.3 %collective-permute-start.2 = (f32[896,128]{1,0:T(8,128)S(1)}, f32[896,128]{1,0:T(8,128)S(1)}, u32[]{:S(2)}, u32[]{:S(2)}) collective-permute-start(f32[896,128]{1,0:T(8,128)S(1)} %bitcast.12), channel_id=1, source_target_pairs={{0,8},{8,0},{1,9},{9,1},{2,10},{10,2},{3,11},{11,3},{4,12},{12,4},... | collective-permute-start | bytes 1376264 | tf_op jit(solution)/shard_map/ppermute | solution.py:489
  106.0 1.4 %collective-permute-done.2.theirs_ref = f32[896,128]{1,0:T(8,128)S(1)} collective-permute-done((f32[896,128]{1,0:T(8,128)S(1)}, f32[896,128]{1,0:T(8,128)S(1)}, u32[]{:S(2)}, u32[]{:S(2)}) %collective-permute-start.2) | collective-permute-done | bytes 458784 | tf_op jit(solution)/shard_map/ppermute | solution.py:489
  107.4 1.0 unpack.1
  (7 shorter events, 0.2 us)
Async XLA Ops:
  0.6 38.4 %copy-start = (f32[3,32,32]{2,1,0:T(8,128)S(1)}, f32[3,32,32]{2,1,0:T(8,128)}, u32[]{:S(2)}) copy-start(f32[3,32,32]{2,1,0:T(8,128)} %qkv_ref.1) | copy-start | bytes 36868
  5.5 4.4 %collective-permute-start = (f32[8,40,128]{2,1,0:T(8,128)S(1)}, f32[8,40,128]{2,1,0:T(8,128)S(1)}, u32[]{:S(2)}, u32[]{:S(2)}) collective-permute-start(f32[8,40,128]{2,1,0:T(8,128)S(1)} %get-tuple-element.31), channel_id=1, source_target_pairs={{0,8},{8,0},{1,9},{9,1},{2,10},{10,2},{3,11},{11,3},{4,12},{12,4},... | collective-permute-start | bytes 491528 | tf_op jit(solution)/shard_map/ppermute | solution.py:489
  59.0 5.9 %collective-permute-start.1 = (f32[896,128]{1,0:T(8,128)S(1)}, f32[896,128]{1,0:T(8,128)S(1)}, u32[]{:S(2)}, u32[]{:S(2)}) collective-permute-start(f32[896,128]{1,0:T(8,128)S(1)} %get-tuple-element.37), channel_id=1, source_target_pairs={{0,8},{8,0},{1,9},{9,1},{2,10},{10,2},{3,11},{11,3},{4,12},{12,4},... | collective-permute-start | bytes 1376264 | tf_op jit(solution)/shard_map/ppermute | solution.py:489
  101.7 5.8 %collective-permute-start.2 = (f32[896,128]{1,0:T(8,128)S(1)}, f32[896,128]{1,0:T(8,128)S(1)}, u32[]{:S(2)}, u32[]{:S(2)}) collective-permute-start(f32[896,128]{1,0:T(8,128)S(1)} %bitcast.12), channel_id=1, source_target_pairs={{0,8},{8,0},{1,9},{9,1},{2,10},{10,2},{3,11},{11,3},{4,12},{12,4},... | collective-permute-start | bytes 1376264 | tf_op jit(solution)/shard_map/ppermute | solution.py:489

commit v2 on v1

--- a/solution.py
+++ b/solution.py
@@ -419,33 +419,51 @@
     )
 
 
-def sum_spread(parts, copies):
+def sum_parts(parts):
     summed = parts[0]
     for k in range(1, parts.shape[0]):
         summed = summed + parts[k]
+    return summed
+
+
+def spread(summed, copies):
     return jnp.broadcast_to(summed[None], (copies,) + summed.shape)
+
+
+def sum_spread(parts, copies):
+    return spread(sum_parts(parts), copies)
 
 
 def unpack_kernel(
     mine_ref,
     theirs_ref,
-    grad_in_ref,
+    grad_in_hbm,
     grad_temp_ref,
     grad_slice_ref,
-    grad_out_ref,
+    grad_out_hbm,
     grad_bias_ref,
     grad_qkv_ref,
+    sems,
 ):
+    def big_copies(first, second):
+        blocks = [(first, k, grad_in_hbm, k) for k in range(3)]
+        blocks += [(second, 0, grad_in_hbm, 3)]
+        blocks += [(second, 1 + k, grad_out_hbm, k) for k in range(2)]
+        return [
+            pltpu.make_async_copy(
+                ref.at[pl.ds(256 * k, 256)], out.at[:, pl.ds(128 * at, 128)], sems.at[i]
+            )
+            for i, (ref, k, out, at) in enumerate(blocks)
+        ]
+
     def unpack(first, second):
-        for k in range(3):
-            grad_in_ref[:, 128 * k : 128 * k + 128] = first[256 * k : 256 * k + 256, :]
-        grad_in_ref[:, 384:512] = second[0:256, :]
+        copies = big_copies(first, second)
+        for copy in copies:
+            copy.start()
         for k in range(4):
             block = first[768 + 32 * k : 800 + 32 * k, :]
             grad_slice_ref[2 * k] = block[:, 0:64]
             grad_slice_ref[2 * k + 1] = pltpu.roll(block, 64, 1)[:, 0:64]
-        grad_out_ref[:, 0:128] = second[256:512, :]
-        grad_out_ref[:, 128:256] = second[512:768, :]
         for k in range(2):
             rows = second[768 + 8 * k : 776 + 8 * k, :]
             grad_temp_ref[:, 128 * k : 128 * k + 128] = rows
@@ -454,6 +472,8 @@
         grad_qkv_ref[0] = qkv[:, 0:32]
         grad_qkv_ref[1] = pltpu.roll(qkv, 96, 1)[:, 0:32]
         grad_qkv_ref[2] = pltpu.roll(qkv, 64, 1)[:, 0:32]
+        for copy in copies:
+            copy.wait()
 
     core = device_place()[2]
 
@@ -468,18 +488,20 @@
 
 def unpack_call(mine, theirs):
     whole = pl.BlockSpec(memory_space=pltpu.VMEM)
+    far = pl.BlockSpec(memory_space=pltpu.HBM)
     return pl.pallas_call(
         unpack_kernel,
         in_specs=[whole, whole],
-        out_specs=[whole] * 6,
+        out_specs=[far, whole, whole, far, whole, whole],
         out_shape=[
-            jax.ShapeDtypeStruct((D, 2 * D), F32),
+            pltpu.HBM((D, 2 * D), F32),
             jax.ShapeDtypeStruct((HEADS, D), F32),
             jax.ShapeDtypeStruct((HEADS, WIDTH, SLICES), F32),
-            jax.ShapeDtypeStruct((D, D), F32),
+            pltpu.HBM((D, D), F32),
             jax.ShapeDtypeStruct((1, D), F32),
             jax.ShapeDtypeStruct((3, WIDTH, WIDTH), F32),
         ],
+        scratch_shapes=[pltpu.SemaphoreType.DMA((6,))],
         compiler_params=pltpu.CompilerParams(vmem_limit_bytes=SMALL_LIMIT),
         name="unpack",
     )(mine, theirs)
@@ -495,9 +517,8 @@
 
 def per_device(points, cotangent, counts, w_in, w_temp, slice_weight, qkv_weight, w_out, b_out):
     packed, *stash = forward_call(counts, points, cotangent, w_in, w_temp, slice_weight, w_out)
-    packed = packed + swap_cores(packed)
-    parts = sum_spread(spread_over(packed, "sub"), 16)
-    parts = spread_over(parts, ("x", "y"))
+    summed = sum_parts(spread_over(packed, "sub"))
+    parts = spread_over(spread(summed + swap_cores(summed), 16), ("x", "y"))
     heads, grad_qkv = attention_call(parts, qkv_weight)
     heads = spread_over(heads, "sub")
     result, grad_points, mine, theirs = backward_call(

time: 109 us -> 110 us (level)
  blocking collectives: 76.7 us -> 78.9 us
  starting transfers between devices: 12.1 us -> 10.2 us
    all_to_all x6, blocking collectives: 76.7 us -> 78.9 us  [spread_over(): return lax.all_to_all(values, axes, 0, 0)]
    ppermute x3, starting transfers between devices: 12.1 us -> 10.2 us  [swap_cores(): return lax.ppermute(values, 'core', [(0, 1), (1, 0)])]
where the time goes in v2:
time: 110 us; the launch traced here: 109 us
  blocking collectives  78.9 us (72%)
  Pallas kernels  15.4 us (14%)
  starting transfers between devices  10.2 us (9%)
  waiting for transfers between devices  3.73 us (3%)
    all_to_all x6, blocking collectives, spread_over(): return lax.all_to_all(values, axes, 0, 0)  78.9 us
    ppermute x3, starting transfers between devices, swap_cores(): return lax.ppermute(values, 'core', [(0, 1), (1, 0)])  10.2 us
    pallas_call x1, Pallas kernels, backward_call(): pl.pallas_call(backward_kernel, in_specs=[pl.BlockSpec(memory_space=pltpu...  7.3 us
    pallas_call x1, Pallas kernels, forward_call(): pl.pallas_call(forward_kernel, in_specs=[pl.BlockSpec(memory_space=pltpu....  4.89 us
    ppermute x3, waiting for transfers between devices, swap_cores(): return lax.ppermute(values, 'core', [(0, 1), (1, 0)])  3.73 us
  transfers between devices with their start and end apart: 3, of which 3 were waited for; matrix products, arithmetic and copies ran while one was open for 0% of the time, Pallas kernels for 0%

profile of v2, /device:TPU:1, one launch (start us, length us, event | category | flops | bytes accessed | tf_op | source)
XLA Modules:
  0.0 109.2 jit_solution(5294684317510512732)
XLA Ops:
  0.6 0.0 copy-start
  0.6 4.9 %forward.1 = (f32[8,40,128]{2,1,0:T(8,128)S(1)}, bf16[256,2048]{1,0:T(8,128)(2,1)S(1)}, f32[8,2048]{1,0:T(8,128)S(1)}, f32[8,2048]{1,0:T(8,128)S(1)}, f32[8,2048...) custom-call(s32[32]{0:T(128)} %counts_ref.3, bf16[2048,256]{1,0:T(8,128)(2,1)} %points_hbm.1, bf16[2048,256]{1,0:T(8,128)(2,1)} %cot_hbm.1, ...), custom_call_target="tpu_custom_call" | custom-call | tf_op jit(solution)/shard_map/forward/pallas_call | solution.py:145
  5.5 17.0 %all_to_all.30 = f32[8,40,128]{2,1,0:T(8,128)S(1)} all-to-all(f32[8,40,128]{2,1,0:T(8,128)S(1)} %get-tuple-element.31), channel_id=1, replica_groups=mesh['x'=4,'y'=4,'core'=2,'sub'=8] {'sub'}, dimensions={0} | all-to-all | bytes 327680 | tf_op jit(solution)/shard_map/all_to_all | solution.py:515
  22.5 2.7 %collective-permute-start = (f32[40,128]{1,0:T(8,128)S(1)}, f32[40,128]{1,0:T(8,128)S(1)}, u32[]{:S(2)}, u32[]{:S(2)}) collective-permute-start(f32[40,128]{1,0:T(8,128)S(1)} %fusion.2), channel_id=1, source_target_pairs={{0,8},{8,0},{1,9},{9,1},{2,10},{10,2},{3,11},{11,3},{4,12},{12,4},... | collective-permute-start | bytes 61448 | tf_op jit(solution)/shard_map/ppermute | solution.py:511
  25.2 0.8 collective-permute-done
  26.1 14.5 %all_to_all.31.parts_ref = f32[16,40,128]{2,1,0:T(8,128)S(1)} all-to-all(f32[16,40,128]{2,1,0:T(8,128)S(1)} %broadcast_in_dim.10), channel_id=1, replica_groups=mesh['x'=4,'y'=4,'core'=2,'sub'=8] {'x','y'}, dimensions={0} | all-to-all | bytes 655360 | tf_op jit(solution)/shard_map/all_to_all | solution.py:515
  40.6 0.0 copy-done
  40.6 1.6 %slice_attention.1 = (f32[8,40,128]{2,1,0:T(8,128)S(1)}, f32[32,128]{1,0:T(8,128)S(1)}) custom-call(f32[16,40,128]{2,1,0:T(8,128)S(1)} %all_to_all.31.parts_ref, f32[3,32,32]{2,1,0:T(8,128)S(1)} %copy-done), custom_call_target="tpu_custom_call" | custom-call | tf_op jit(solution)/shard_map/slice_attention/pallas_call | solution.py:212
  42.3 10.8 %all_to_all.32.heads_ref = f32[8,40,128]{2,1,0:T(8,128)S(1)} all-to-all(f32[8,40,128]{2,1,0:T(8,128)S(1)} %get-tuple-element.32), channel_id=1, replica_groups=mesh['x'=4,'y'=4,'core'=2,'sub'=8] {'sub'}, dimensions={0} | all-to-all | bytes 327680 | tf_op jit(solution)/shard_map/all_to_all | solution.py:515
  53.0 7.3 %backward.1 = (bf16[2048,256]{1,0:T(8,128)(2,1)}, bf16[2048,256]{1,0:T(8,128)(2,1)}, f32[896,128]{1,0:T(8,128)S(1)}, f32[896,128]{1,0:T(8,128)S(1)}) custom-call(s32[32]{0:T(128)} %counts_ref.3, bf16[2048,256]{1,0:T(8,128)(2,1)} %points_hbm.1, bf16[2048,256]{1,0:T(8,128)(2,1)} %cot_hbm.1, bf16[256,2048]{1,0:T(8,128)(2,1)S(1)} %get-tuple-element.26.fx_ref, ...), custom_call_target="tpu_custom_call" | custom-call | tf_op jit(solution)/shard_map/backward/pallas_call | solution.py:385
  60.3 3.3 %collective-permute-start.1 = (f32[896,128]{1,0:T(8,128)S(1)}, f32[896,128]{1,0:T(8,128)S(1)}, u32[]{:S(2)}, u32[]{:S(2)}) collective-permute-start(f32[896,128]{1,0:T(8,128)S(1)} %get-tuple-element.37), channel_id=1, source_target_pairs={{0,8},{8,0},{1,9},{9,1},{2,10},{10,2},{3,11},{11,3},{4,12},{12,4},... | collective-permute-start | bytes 1376264 | tf_op jit(solution)/shard_map/ppermute | solution.py:511
  63.6 1.4 %collective-permute-done.1 = f32[896,128]{1,0:T(8,128)S(1)} collective-permute-done((f32[896,128]{1,0:T(8,128)S(1)}, f32[896,128]{1,0:T(8,128)S(1)}, u32[]{:S(2)}, u32[]{:S(2)}) %collective-permute-start.1) | collective-permute-done | bytes 458784 | tf_op jit(solution)/shard_map/ppermute | solution.py:511
  65.0 0.1 add.130
  65.1 13.0 %all_to_all.33 = f32[16,56,128]{2,1,0:T(8,128)S(1)} all-to-all(f32[16,56,128]{2,1,0:T(8,128)S(1)} %bitcast.16), channel_id=1, replica_groups=mesh['x'=4,'y'=4,'core'=2,'sub'=8] {'x','y'}, dimensions={0} | all-to-all | bytes 917504 | tf_op jit(solution)/shard_map/all_to_all | solution.py:515
  78.2 11.3 %all_to_all.34 = f32[8,56,128]{2,1,0:T(8,128)S(1)} all-to-all(f32[8,56,128]{2,1,0:T(8,128)S(1)} %broadcast_in_dim.24), channel_id=1, replica_groups=mesh['x'=4,'y'=4,'core'=2,'sub'=8] {'sub'}, dimensions={0} | all-to-all | bytes 458752 | tf_op jit(solution)/shard_map/all_to_all | solution.py:515
  89.5 12.3 %all_to_all.35 = f32[16,56,128]{2,1,0:T(8,128)S(1)} all-to-all(f32[16,56,128]{2,1,0:T(8,128)S(1)} %broadcast_in_dim.26), channel_id=1, replica_groups=mesh['x'=4,'y'=4,'core'=2,'sub'=8] {'x','y'}, dimensions={0} | all-to-all | bytes 917504 | tf_op jit(solution)/shard_map/all_to_all | solution.py:515
  101.8 4.3 %collective-permute-start.2 = (f32[896,128]{1,0:T(8,128)S(1)}, f32[896,128]{1,0:T(8,128)S(1)}, u32[]{:S(2)}, u32[]{:S(2)}) collective-permute-start(f32[896,128]{1,0:T(8,128)S(1)} %bitcast.14), channel_id=1, source_target_pairs={{0,8},{8,0},{1,9},{9,1},{2,10},{10,2},{3,11},{11,3},{4,12},{12,4},... | collective-permute-start | bytes 1376264 | tf_op jit(solution)/shard_map/ppermute | solution.py:511
  106.1 1.4 %collective-permute-done.2.theirs_ref = f32[896,128]{1,0:T(8,128)S(1)} collective-permute-done((f32[896,128]{1,0:T(8,128)S(1)}, f32[896,128]{1,0:T(8,128)S(1)}, u32[]{:S(2)}, u32[]{:S(2)}) %collective-permute-start.2) | collective-permute-done | bytes 458784 | tf_op jit(solution)/shard_map/ppermute | solution.py:511
  107.6 1.6 %unpack.1 = (f32[256,512]{1,0:T(8,128)}, f32[8,256]{1,0:T(8,128)}, f32[8,32,64]{2,1,0:T(8,128)}, f32[256,256]{1,0:T(8,128)}, f32[1,256]{1,0:T(1,128)}, /*index=5*/f32[3,32,32]{2,1,0:T(8,128)}) custom-call(f32[896,128]{1,0:T(8,128)S(1)} %bitcast.15, f32[896,128]{1,0:T(8,128)S(1)} %collective-permute-done.2.theirs_ref), custom_call_target="tpu_custom_call" | custom-call | tf_op jit(solution)/shard_map/unpack/pallas_call | solution.py:492
  (7 shorter events, 0.1 us)
Async XLA Ops:
  0.6 40.0 %copy-start = (f32[3,32,32]{2,1,0:T(8,128)S(1)}, f32[3,32,32]{2,1,0:T(8,128)}, u32[]{:S(2)}) copy-start(f32[3,32,32]{2,1,0:T(8,128)} %qkv_ref.1) | copy-start | bytes 36868
  22.5 3.5 %collective-permute-start = (f32[40,128]{1,0:T(8,128)S(1)}, f32[40,128]{1,0:T(8,128)S(1)}, u32[]{:S(2)}, u32[]{:S(2)}) collective-permute-start(f32[40,128]{1,0:T(8,128)S(1)} %fusion.2), channel_id=1, source_target_pairs={{0,8},{8,0},{1,9},{9,1},{2,10},{10,2},{3,11},{11,3},{4,12},{12,4},... | collective-permute-start | bytes 61448 | tf_op jit(solution)/shard_map/ppermute | solution.py:511
  60.3 4.7 %collective-permute-start.1 = (f32[896,128]{1,0:T(8,128)S(1)}, f32[896,128]{1,0:T(8,128)S(1)}, u32[]{:S(2)}, u32[]{:S(2)}) collective-permute-start(f32[896,128]{1,0:T(8,128)S(1)} %get-tuple-element.37), channel_id=1, source_target_pairs={{0,8},{8,0},{1,9},{9,1},{2,10},{10,2},{3,11},{11,3},{4,12},{12,4},... | collective-permute-start | bytes 1376264 | tf_op jit(solution)/shard_map/ppermute | solution.py:511
  101.8 5.8 %collective-permute-start.2 = (f32[896,128]{1,0:T(8,128)S(1)}, f32[896,128]{1,0:T(8,128)S(1)}, u32[]{:S(2)}, u32[]{:S(2)}) collective-permute-start(f32[896,128]{1,0:T(8,128)S(1)} %bitcast.14), channel_id=1, source_target_pairs={{0,8},{8,0},{1,9},{9,1},{2,10},{10,2},{3,11},{11,3},{4,12},{12,4},... | collective-permute-start | bytes 1376264 | tf_op jit(solution)/shard_map/ppermute | solution.py:511

commit v3 on v1

--- a/solution.py
+++ b/solution.py
@@ -189,22 +189,20 @@
     grad_scores = weights * (grad_weights - inner) * scale
     grad_query = nn(grad_scores, keys, HIGH)
     grad_keys = tn(grad_scores, query, HIGH)
-    grad_tokens = (
-        nt(grad_query, w_q, HIGH) + nt(grad_keys, w_k, HIGH) + nt(grad_values, w_v, HIGH)
-    )
+    grads = jnp.concatenate([grad_query, grad_keys, grad_values], axis=1)
+    grad_tokens = nt(grads, jnp.concatenate([w_q, w_k, w_v], axis=1), HIGH)
     grad_qkv_ref[...] = jnp.zeros_like(grad_qkv_ref)
-    for i, grad in enumerate((grad_query, grad_keys, grad_values)):
-        grad_qkv_ref[:, WIDTH * i : WIDTH * i + WIDTH] = tn(tokens, grad, HIGH) * (1.0 / 32)
+    grad_qkv_ref[:, 0 : 3 * WIDTH] = tn(tokens, grads, HIGH) * (1.0 / 32)
     grad_numer = grad_tokens * inv
     grad_totals = -jnp.sum(grad_tokens * tokens, axis=1, keepdims=True) * inv
     grad_row = jnp.broadcast_to(grad_totals, (SLICES, 128)).T[0:8]
+    block = jnp.concatenate(
+        [attended[0:32], grad_numer[0:32], attended[32:64], grad_numer[32:64]], axis=1
+    )
+    rows = jnp.concatenate([grad_row, grad_row], axis=1)
     for k in range(out_ref.shape[0]):
-        out_ref[k, 0:32, 0:32] = attended[0:32]
-        out_ref[k, 0:32, 32:64] = grad_numer[0:32]
-        out_ref[k, 0:32, 64:96] = attended[32:64]
-        out_ref[k, 0:32, 96:128] = grad_numer[32:64]
-        out_ref[k, 32:40, 0:64] = grad_row
-        out_ref[k, 32:40, 64:128] = grad_row
+        out_ref[k, 0:32, :] = block
+        out_ref[k, 32:40, :] = rows
 
 
 def attention_call(parts, qkv_weight):

time: 109 us -> 109 us (level)
  no operation moved by 1% of the time
where the time goes in v3:
time: 109 us; the launch traced here: 108 us
  blocking collectives  76.6 us (70%)
  Pallas kernels  14.8 us (14%)
  starting transfers between devices  12.1 us (11%)
  waiting for transfers between devices  3.91 us (4%)
    all_to_all x6, blocking collectives, spread_over(): return lax.all_to_all(values, axes, 0, 0)  76.6 us
    ppermute x3, starting transfers between devices, swap_cores(): return lax.ppermute(values, 'core', [(0, 1), (1, 0)])  12.1 us
    pallas_call x1, Pallas kernels, backward_call(): pl.pallas_call(backward_kernel, in_specs=[pl.BlockSpec(memory_space=pltpu...  7.29 us
    pallas_call x1, Pallas kernels, forward_call(): pl.pallas_call(forward_kernel, in_specs=[pl.BlockSpec(memory_space=pltpu....  4.89 us
    ppermute x3, waiting for transfers between devices, swap_cores(): return lax.ppermute(values, 'core', [(0, 1), (1, 0)])  3.91 us
  transfers between devices with their start and end apart: 3, of which 3 were waited for; matrix products, arithmetic and copies ran while one was open for 0% of the time, Pallas kernels for 0%

profile of v3, /device:TPU:1, one launch (start us, length us, event | category | flops | bytes accessed | tf_op | source)
XLA Modules:
  0.0 108.4 jit_solution(4254819034158224199)
XLA Ops:
  0.6 0.0 copy-start
  0.6 4.9 %forward.1 = (f32[8,40,128]{2,1,0:T(8,128)S(1)}, bf16[256,2048]{1,0:T(8,128)(2,1)S(1)}, f32[8,2048]{1,0:T(8,128)S(1)}, f32[8,2048]{1,0:T(8,128)S(1)}, f32[8,2048...) custom-call(s32[32]{0:T(128)} %counts_ref.3, bf16[2048,256]{1,0:T(8,128)(2,1)} %points_hbm.1, bf16[2048,256]{1,0:T(8,128)(2,1)} %cot_hbm.1, ...), custom_call_target="tpu_custom_call" | custom-call | tf_op jit(solution)/shard_map/forward/pallas_call | solution.py:145
  5.5 3.3 %collective-permute-start = (f32[8,40,128]{2,1,0:T(8,128)S(1)}, f32[8,40,128]{2,1,0:T(8,128)S(1)}, u32[]{:S(2)}, u32[]{:S(2)}) collective-permute-start(f32[8,40,128]{2,1,0:T(8,128)S(1)} %get-tuple-element.31), channel_id=1, source_target_pairs={{0,8},{8,0},{1,9},{9,1},{2,10},{10,2},{3,11},{11,3},{4,12},{12,4},... | collective-permute-start | bytes 491528 | tf_op jit(solution)/shard_map/ppermute | solution.py:487
  8.9 1.0 collective-permute-done
  9.9 14.9 %all_to_all.30 = f32[8,40,128]{2,1,0:T(8,128)S(1)} all-to-all(f32[8,40,128]{2,1,0:T(8,128)S(1)} %add.122), channel_id=1, replica_groups=mesh['x'=4,'y'=4,'core'=2,'sub'=8] {'sub'}, dimensions={0} | all-to-all | bytes 327680 | tf_op jit(solution)/shard_map/all_to_all | solution.py:491
  24.8 14.2 %all_to_all.31.parts_ref = f32[16,40,128]{2,1,0:T(8,128)S(1)} all-to-all(f32[16,40,128]{2,1,0:T(8,128)S(1)} %broadcast_in_dim.25), channel_id=1, replica_groups=mesh['x'=4,'y'=4,'core'=2,'sub'=8] {'x','y'}, dimensions={0} | all-to-all | bytes 655360 | tf_op jit(solution)/shard_map/all_to_all | solution.py:491
  39.1 0.0 copy-done
  39.1 1.6 %slice_attention.1 = (f32[8,40,128]{2,1,0:T(8,128)S(1)}, f32[32,128]{1,0:T(8,128)S(1)}) custom-call(f32[16,40,128]{2,1,0:T(8,128)S(1)} %all_to_all.31.parts_ref, f32[3,32,32]{2,1,0:T(8,128)S(1)} %copy-done), custom_call_target="tpu_custom_call" | custom-call | tf_op jit(solution)/shard_map/slice_attention/pallas_call | solution.py:210
  40.7 11.0 %all_to_all.32.heads_ref = f32[8,40,128]{2,1,0:T(8,128)S(1)} all-to-all(f32[8,40,128]{2,1,0:T(8,128)S(1)} %get-tuple-element.32), channel_id=1, replica_groups=mesh['x'=4,'y'=4,'core'=2,'sub'=8] {'sub'}, dimensions={0} | all-to-all | bytes 327680 | tf_op jit(solution)/shard_map/all_to_all | solution.py:491
  51.6 7.3 %backward.1 = (bf16[2048,256]{1,0:T(8,128)(2,1)}, bf16[2048,256]{1,0:T(8,128)(2,1)}, f32[896,128]{1,0:T(8,128)S(1)}, f32[896,128]{1,0:T(8,128)S(1)}) custom-call(s32[32]{0:T(128)} %counts_ref.3, bf16[2048,256]{1,0:T(8,128)(2,1)} %points_hbm.1, bf16[2048,256]{1,0:T(8,128)(2,1)} %cot_hbm.1, bf16[256,2048]{1,0:T(8,128)(2,1)S(1)} %get-tuple-element.26.fx_ref, ...), custom_call_target="tpu_custom_call" | custom-call | tf_op jit(solution)/shard_map/backward/pallas_call | solution.py:383
  58.9 4.5 %collective-permute-start.1 = (f32[896,128]{1,0:T(8,128)S(1)}, f32[896,128]{1,0:T(8,128)S(1)}, u32[]{:S(2)}, u32[]{:S(2)}) collective-permute-start(f32[896,128]{1,0:T(8,128)S(1)} %get-tuple-element.37), channel_id=1, source_target_pairs={{0,8},{8,0},{1,9},{9,1},{2,10},{10,2},{3,11},{11,3},{4,12},{12,4},... | collective-permute-start | bytes 1376264 | tf_op jit(solution)/shard_map/ppermute | solution.py:487
  63.4 1.4 %collective-permute-done.1 = f32[896,128]{1,0:T(8,128)S(1)} collective-permute-done((f32[896,128]{1,0:T(8,128)S(1)}, f32[896,128]{1,0:T(8,128)S(1)}, u32[]{:S(2)}, u32[]{:S(2)}) %collective-permute-start.1) | collective-permute-done | bytes 458784 | tf_op jit(solution)/shard_map/ppermute | solution.py:487
  64.8 0.1 add.130
  64.9 13.0 %all_to_all.33 = f32[16,56,128]{2,1,0:T(8,128)S(1)} all-to-all(f32[16,56,128]{2,1,0:T(8,128)S(1)} %bitcast.14), channel_id=1, replica_groups=mesh['x'=4,'y'=4,'core'=2,'sub'=8] {'x','y'}, dimensions={0} | all-to-all | bytes 917504 | tf_op jit(solution)/shard_map/all_to_all | solution.py:491
  78.0 11.3 %all_to_all.34 = f32[8,56,128]{2,1,0:T(8,128)S(1)} all-to-all(f32[8,56,128]{2,1,0:T(8,128)S(1)} %broadcast_in_dim.27), channel_id=1, replica_groups=mesh['x'=4,'y'=4,'core'=2,'sub'=8] {'sub'}, dimensions={0} | all-to-all | bytes 458752 | tf_op jit(solution)/shard_map/all_to_all | solution.py:491
  89.3 12.3 %all_to_all.35 = f32[16,56,128]{2,1,0:T(8,128)S(1)} all-to-all(f32[16,56,128]{2,1,0:T(8,128)S(1)} %broadcast_in_dim.29), channel_id=1, replica_groups=mesh['x'=4,'y'=4,'core'=2,'sub'=8] {'x','y'}, dimensions={0} | all-to-all | bytes 917504 | tf_op jit(solution)/shard_map/all_to_all | solution.py:491
  101.6 4.3 %collective-permute-start.2 = (f32[896,128]{1,0:T(8,128)S(1)}, f32[896,128]{1,0:T(8,128)S(1)}, u32[]{:S(2)}, u32[]{:S(2)}) collective-permute-start(f32[896,128]{1,0:T(8,128)S(1)} %bitcast.12), channel_id=1, source_target_pairs={{0,8},{8,0},{1,9},{9,1},{2,10},{10,2},{3,11},{11,3},{4,12},{12,4},... | collective-permute-start | bytes 1376264 | tf_op jit(solution)/shard_map/ppermute | solution.py:487
  106.0 1.4 %collective-permute-done.2.theirs_ref = f32[896,128]{1,0:T(8,128)S(1)} collective-permute-done((f32[896,128]{1,0:T(8,128)S(1)}, f32[896,128]{1,0:T(8,128)S(1)}, u32[]{:S(2)}, u32[]{:S(2)}) %collective-permute-start.2) | collective-permute-done | bytes 458784 | tf_op jit(solution)/shard_map/ppermute | solution.py:487
  107.4 1.0 unpack.1
  (7 shorter events, 0.2 us)
Async XLA Ops:
  0.6 38.4 %copy-start = (f32[3,32,32]{2,1,0:T(8,128)S(1)}, f32[3,32,32]{2,1,0:T(8,128)}, u32[]{:S(2)}) copy-start(f32[3,32,32]{2,1,0:T(8,128)} %qkv_ref.1) | copy-start | bytes 36868
  5.5 4.4 %collective-permute-start = (f32[8,40,128]{2,1,0:T(8,128)S(1)}, f32[8,40,128]{2,1,0:T(8,128)S(1)}, u32[]{:S(2)}, u32[]{:S(2)}) collective-permute-start(f32[8,40,128]{2,1,0:T(8,128)S(1)} %get-tuple-element.31), channel_id=1, source_target_pairs={{0,8},{8,0},{1,9},{9,1},{2,10},{10,2},{3,11},{11,3},{4,12},{12,4},... | collective-permute-start | bytes 491528 | tf_op jit(solution)/shard_map/ppermute | solution.py:487
  58.9 5.9 %collective-permute-start.1 = (f32[896,128]{1,0:T(8,128)S(1)}, f32[896,128]{1,0:T(8,128)S(1)}, u32[]{:S(2)}, u32[]{:S(2)}) collective-permute-start(f32[896,128]{1,0:T(8,128)S(1)} %get-tuple-element.37), channel_id=1, source_target_pairs={{0,8},{8,0},{1,9},{9,1},{2,10},{10,2},{3,11},{11,3},{4,12},{12,4},... | collective-permute-start | bytes 1376264 | tf_op jit(solution)/shard_map/ppermute | solution.py:487
  101.6 5.8 %collective-permute-start.2 = (f32[896,128]{1,0:T(8,128)S(1)}, f32[896,128]{1,0:T(8,128)S(1)}, u32[]{:S(2)}, u32[]{:S(2)}) collective-permute-start(f32[896,128]{1,0:T(8,128)S(1)} %bitcast.12), channel_id=1, source_target_pairs={{0,8},{8,0},{1,9},{9,1},{2,10},{10,2},{3,11},{11,3},{4,12},{12,4},... | collective-permute-start | bytes 1376264 | tf_op jit(solution)/shard_map/ppermute | solution.py:487
